TPU v7x, 256 devices: a whole 4x4x8 slice. The times are simulated.
256 devices in a mesh: section: 2 (over z_hi), grp: 8 (over z_lo, core), tp: 16 (over x, y).
Axes of the slice: x: 4, y: 4, z: 8 (z_hi: 2, z_lo: 4; z = z_hi * 4 + z_lo), core: 2. Of those that a mesh axis runs over, the one named last changes fastest.
Arguments:
- heads_in: bfloat16 [2, 3072, 8192], P('section', 'grp', 'tp'), may hold values from -6 to 6
- weights: bfloat16 [2, 8192, 8192], P('section', 'tp'), may hold values from -0.0625 to 0.0625
- residual: bfloat16 [3072, 8192], P(('grp', 'tp')), may hold values from -50 to 50
- norm_gain: float32 [8192], replicated, may hold values from 0.1 to 1.9
Outputs:
- heads_out: bfloat16 [2, 3072, 8192], P('section', 'grp', 'tp')
- weight_grad: float32 [2, 8192, 8192], P('section', 'grp', 'tp')
- boundary_grad: bfloat16 [3072, 8192], P(('grp', 'tp'))
- gain_grad: float32 [8192], replicated
All inputs are finite; a program needn't handle non-finite values.
Results may differ from a plain program's by a relative error of at most 0.027.
Values may be sent and summed in bfloat16 or wider, within the bound.
A program may use at most 128 MiB of HBM per device.

v0:
```python
import math

import jax
import jax.numpy as jnp
from jax import lax
from jax.experimental import pallas as pl
from jax.experimental.pallas import tpu as pltpu
from jax.sharding import PartitionSpec as P

EPSILON = 1e-05
MESH = pl.DeviceIdType.MESH

SIDE = 4
GROUPS = 8
UNITS = 8
FAR_UNITS = 5
CHUNKS = 2 * UNITS
FAR_CHUNKS = 2 * FAR_UNITS
WIDE = 256
HALF = WIDE // 2
UNIT_WIDE = 2 * WIDE
SHARD = 2 * UNIT_WIDE
OWN = 24
TALL = 2 * OWN
SLOTS = GROUPS - 1
GAIN_STEPS = 7


def lower_start(t, h=0):
    return pl.multiple_of(t * UNIT_WIDE + h * WIDE, WIDE)


def upper_start(t, h=0):
    return pl.multiple_of((GROUPS - 1 - t // 2) * SHARD + (t % 2) * UNIT_WIDE + h * WIDE, WIDE)


def plane_device(h, first, second):
    x, y = (first, second) if h == 0 else (second, first)
    return {"tp": x * SIDE + y}


def stacked(*parts):
    return jnp.concatenate(parts, axis=0)


def both_halves(row_pair):
    total = row_pair[:OWN] + row_pair[OWN:]
    return stacked(total, total)


def lanes(value):
    return sum(value[:, 128 * i : 128 * (i + 1)] for i in range(value.shape[1] // 128))


def wide(value):
    return value.astype(jnp.float32)


def narrow(value):
    return value.astype(jnp.bfloat16)


def remote(source, target, send_sem, recv_sem, device):
    return pltpu.make_async_remote_copy(
        src_ref=source,
        dst_ref=target,
        send_sem=send_sem,
        recv_sem=recv_sem,
        device_id=device,
        device_id_type=MESH,
    )


def greet(peers):
    barrier = pltpu.get_barrier_semaphore()
    for peer in peers:
        pl.semaphore_signal(barrier, inc=1, device_id=peer, device_id_type=MESH)
    pl.semaphore_wait(barrier, len(peers))


def boundary_kernel(
    heads_in, weights, residual_in, gain_in, heads_out, grads_out, grad_out, gain_out,
    heads, residual, gain, heads_done, grads, own_grad, gain_done,
    heads_t, grads_t, weight_buf, part, from1, from2, from3, from4, both,
    values, columns, exchange, tokens, column_tokens, from_near, heads_all, heads_total, gain_own, gain_got,
    input_sem, output_sem, weight_sem, send_sem, recv_sem, value_send, value_recv, column_send, column_recv,
    exchange_send, exchange_recv, heads_send, heads_recv, near_send, near_recv, gain_send, gain_recv,
):
    tp = lax.axis_index("tp")
    x, y = tp // SIDE, tp % SIDE
    section = lax.axis_index("section")
    group = lax.axis_index("grp")
    z, core = group // 2, group % 2
    other = {"section": 1 - section}
    sibling_group = 2 * z + 1 - core
    sibling = {"grp": sibling_group}
    next_plane = z + 1 - 2 * (z % 2)
    rows_dev, depth = heads.shape
    grad_scale = 1.0 / math.sqrt(rows_dev * GROUPS)

    def axes(h):
        return (x, y) if h == 0 else (y, x)

    def wait_arrived(size, sem):
        remote(size, size, heads_send.at[0], sem, sibling).wait_recv()

    def wait_sent(size, sem):
        remote(size, size, sem, heads_recv.at[0], sibling).wait_send()

    def weight_copy(t, upper):
        cols = pl.ds(upper_start(t) if upper else lower_start(t), UNIT_WIDE)
        return pltpu.make_async_copy(
            weights.at[:, cols], weight_buf.at[:, cols], weight_sem.at[t, upper]
        )

    def start_weights(t, carry):
        weight_copy(t, 0).start()
        weight_copy(t, 1).start()
        return carry

    heads_load, residual_load, gain_load = [
        pltpu.make_async_copy(source, target, input_sem.at[at])
        for at, (source, target) in enumerate(
            ((heads_in, heads), (residual_in, residual), (gain_in, gain))
        )
    ]
    heads_load.start()
    lax.fori_loop(0, UNITS, start_weights, 0)
    residual_load.start()
    gain_load.start()
    greet(
        [plane_device(0, (x + step) % SIDE, y) for step in (1, 3)]
        + [plane_device(0, x, (y + step) % SIDE) for step in (1, 3)]
        + [other, sibling]
        + [{"grp": 2 * ((z + hop) % SIDE) + k} for hop in range(1, SIDE) for k in range(2)]
    )
    heads_load.wait()

    def plane_slot(origin, at):
        return 2 * ((origin + SIDE - 1 - at) % SIDE)

    def heads_arrived(slot):
        remote(
            heads_t, heads_all.at[slot], heads_send.at[SLOTS - 1], heads_recv.at[slot], sibling
        ).wait_recv()

    def sibling_heads():
        slot = SLOTS - 1
        return remote(
            heads_t, heads_all.at[slot], heads_send.at[slot], heads_recv.at[slot], sibling
        )

    relays = ((1, 0), (-1, 0), (1, 1), (-1, 1), (1, 2), (-1, 2))

    def each_relay(wanted, act):
        for at, (step, away) in enumerate(relays):
            if away not in wanted:
                continue
            first, last = (away, SIDE - 2) if step > 0 else (1, SIDE - 1 - away)

            @pl.when(jnp.logical_and(z >= first, z <= last))
            def _():
                origin, target = z - step * away, z + step
                held = plane_slot(origin, z) + core
                slot = plane_slot(origin, target) + core
                act(
                    remote(
                        heads_all.at[held] if away else heads_t,
                        heads_all.at[slot],
                        heads_send.at[SLOTS + at],
                        heads_recv.at[slot],
                        {"grp": 2 * target + core},
                    ),
                    held,
                )

    def start_relay(relay, held):
        relay.start()

    def pass_relay(relay, held):
        heads_arrived(held)
        relay.start()

    def passed_heads(j):
        slot = 2 * j + core
        held = heads_all.at[slot]
        return remote(held, held, heads_send.at[slot], heads_recv.at[slot], sibling)

    def pass_heads():
        @pl.when(jnp.logical_or(z == 0, z == SIDE - 1))
        def _():
            for j in range(SIDE - 1):
                heads_arrived(2 * j + core)

        for j in range(SIDE - 1):
            passed_heads(j).start()

    def send_heads():
        heads_t[...] = heads[...].T
        each_relay((0,), start_relay)
        sibling_heads().start()


    def copy(u, h, step):
        chunk = 2 * u + h
        a, b = axes(h)
        right, left = (a + 1) % SIDE, (a + 3) % SIDE
        up, down = (b + 1) % SIDE, (b + 3) % SIDE
        low, high = pl.ds(0, HALF), pl.ds(HALF, HALF)
        far_a, far_b = (a + 2) % SIDE, (b + 2) % SIDE
        source, target, device = [
            lambda: (part.at[chunk, far_a, :, :, low], from1.at[chunk, 0], plane_device(h, right, b)),
            lambda: (part.at[chunk, far_a, :, :, high], from1.at[chunk, 1], plane_device(h, left, b)),
            lambda: (part.at[chunk, right], from2.at[chunk, 0], plane_device(h, right, b)),
            lambda: (part.at[chunk, left], from2.at[chunk, 1], plane_device(h, left, b)),
            lambda: (part.at[chunk, a, far_b, :, low], from3.at[chunk, 0], plane_device(h, a, up)),
            lambda: (part.at[chunk, a, far_b, :, high], from3.at[chunk, 1], plane_device(h, a, down)),
            lambda: (part.at[chunk, a, up], from4.at[chunk, 0], plane_device(h, a, up)),
            lambda: (part.at[chunk, a, down], from4.at[chunk, 1], plane_device(h, a, down)),
            lambda: (both.at[section, chunk], both.at[section, chunk], other),
        ][step]()
        return remote(source, target, send_sem.at[u], recv_sem.at[u, step // 2], device)

    reduce_sizes = [
        part.at[0, 0:2], part.at[0], part.at[0, 0, 0:2], part.at[0, 0], part.at[0, 0, 0:2]
    ]

    def arrive(u, stage):
        wait_arrived(reduce_sizes[stage], recv_sem.at[u, stage])

    def multiply(u):
        weight_copy(u, 0).wait()
        weight_copy(u, 1).wait()
        lower, upper = [
            jnp.dot(
                heads[...], weight_buf[:, pl.ds(start, UNIT_WIDE)],
                preferred_element_type=jnp.float32,
            )
            for start in (lower_start(u), upper_start(u))
        ]
        for h in range(2):
            cols = slice(h * WIDE, (h + 1) * WIDE)
            for i in range(SIDE * SIDE):
                rows = slice(OWN * i, OWN * (i + 1))
                a, b = (i // SIDE, i % SIDE) if h == 0 else (i % SIDE, i // SIDE)
                part[2 * u + h, a, b] = narrow(stacked(lower[rows, cols], upper[rows, cols]))
            copy(u, h, 0).start()
            copy(u, h, 1).start()

    def near_first(u):
        arrive(u, 0)
        for h in range(2):
            chunk = 2 * u + h
            a, b = axes(h)
            right, left = (a + 1) % SIDE, (a + 3) % SIDE
            part[chunk, right, :, :, :HALF] = narrow(
                wide(part[chunk, right, :, :, :HALF]) + wide(from1[chunk, 0])
            )
            copy(u, h, 2).start()
            part[chunk, left, :, :, HALF:] = narrow(
                wide(part[chunk, left, :, :, HALF:]) + wide(from1[chunk, 1])
            )
            copy(u, h, 3).start()

    def far_second(u):
        arrive(u, 1)
        for h in range(2):
            chunk = 2 * u + h
            a, b = axes(h)
            part[chunk, a] = narrow(
                wide(part[chunk, a]) + (wide(from2[chunk, 0]) + wide(from2[chunk, 1]))
            )
            copy(u, h, 4).start()
            copy(u, h, 5).start()

    def near_second(u):
        arrive(u, 2)
        for h in range(2):
            chunk = 2 * u + h
            a, b = axes(h)
            up, down = (b + 1) % SIDE, (b + 3) % SIDE
            part[chunk, a, up, :, :HALF] = narrow(
                wide(part[chunk, a, up, :, :HALF]) + wide(from3[chunk, 0])
            )
            copy(u, h, 6).start()
            part[chunk, a, down, :, HALF:] = narrow(
                wide(part[chunk, a, down, :, HALF:]) + wide(from3[chunk, 1])
            )
            copy(u, h, 7).start()

    def finish(u):
        arrive(u, 3)
        for h in range(2):
            chunk = 2 * u + h
            a, b = axes(h)
            total = wide(part[chunk, a, b]) + (wide(from4[chunk, 0]) + wide(from4[chunk, 1]))
            rows = stacked(
                wide(residual[:, pl.ds(lower_start(u, h), WIDE)]),
                wide(residual[:, pl.ds(upper_start(u, h), WIDE)]),
            )
            total = total + jnp.where(section == 0, rows, 0.0)
            both[section, chunk] = narrow(total)
            copy(u, h, 8).start()

    def within(value, count):
        return jnp.logical_and(value >= 0, value < count)

    stages = (multiply, near_first, far_second, near_second, finish)

    def reduce_turn(n, carry):
        for late, stage in enumerate(stages):

            @pl.when(within(n - late, UNITS))
            def _():
                stage(n - late)

        @pl.when(n == 1)
        def _():
            send_heads()

        @pl.when(n == UNITS - 1)
        def _():
            each_relay((1,), pass_relay)

        return carry

    residual_load.wait()
    gain_load.wait()
    lax.fori_loop(0, UNITS + len(stages) - 1, reduce_turn, 0)
    heads_total[...] = jnp.zeros_like(heads_total)
    grads_t[...] = jnp.zeros_like(grads_t)


    def gather_of(store, sends, recvs):
        half = store.shape[-1] // 2

        def gather(p, h, step):
            chunk = 2 * p + h
            a, b = axes(h)
            right, left = (a + 1) % SIDE, (a + 3) % SIDE
            up, down = (b + 1) % SIDE, (b + 3) % SIDE
            low, high = pl.ds(0, half), pl.ds(half, half)
            block, device = [
                lambda: (store.at[chunk, b, a], plane_device(h, right, b)),
                lambda: (store.at[chunk, b, a], plane_device(h, left, b)),
                lambda: (store.at[chunk, b, left, :, low], plane_device(h, right, b)),
                lambda: (store.at[chunk, b, right, :, high], plane_device(h, left, b)),
                lambda: (store.at[chunk, b], plane_device(h, a, up)),
                lambda: (store.at[chunk, b], plane_device(h, a, down)),
                lambda: (store.at[chunk, down, :, :, low], plane_device(h, a, up)),
                lambda: (store.at[chunk, up, :, :, high], plane_device(h, a, down)),
            ][step]()
            return remote(block, block, sends.at[p], recvs.at[p, step // 2], device)

        return gather

    gather_values = gather_of(values, value_send, value_recv)
    gather_columns = gather_of(columns, column_send, column_recv)

    gather_sizes = [values.at[0, 0], values.at[0, 0, 0:2], values.at[0], values.at[0, 0:2]]

    def exchanged(target, e):
        unit = 2 * (z % 2) + e if e < 2 else FAR_UNITS - 1
        a, b = x + core * (y - x), y + core * (x - y)
        return remote(
            exchange.at[target, e],
            columns.at[2 * unit + core, b, a],
            exchange_send.at[0],
            exchange_recv.at[unit],
            {"grp": target},
        )

    def gain_rows(t, h):
        return stacked(
            jnp.broadcast_to(gain[:, pl.ds(lower_start(t, h), WIDE)], (OWN, WIDE)),
            jnp.broadcast_to(gain[:, pl.ds(upper_start(t, h), WIDE)], (OWN, WIDE)),
        )

    zero = jnp.zeros((TALL, 128), jnp.float32)

    def row_mean(total):
        return both_halves(jnp.sum(total, axis=1, keepdims=True)) / (GROUPS * SHARD)

    def add_sums(t, total):
        arrive(t, 4)
        for h in range(2):
            total = total + lanes(wide(both[0, 2 * t + h]))
        return total

    mean = row_mean(lax.fori_loop(0, UNITS, add_sums, zero))

    def add_squares(t, total):
        for h in range(2):
            centred = wide(both[0, 2 * t + h]) - mean
            total = total + lanes(centred * centred)
        return total

    inv_scale = lax.rsqrt(row_mean(lax.fori_loop(0, UNITS, add_squares, zero)) + EPSILON)

    def add_means(t, totals):
        for h in range(2):
            unit = (wide(both[0, 2 * t + h]) - mean) * inv_scale
            scaled = gain_rows(t, h) * wide(both[1, 2 * t + h])
            totals = (totals[0] + lanes(scaled), totals[1] + lanes(scaled * unit))
        return totals

    sums = lax.fori_loop(0, UNITS, add_means, (zero, zero))
    mean_scaled, mean_product = row_mean(sums[0]), row_mean(sums[1])
    first_unit = SIDE * ((z // 2 + z % 2 + 1) % 2)

    def write(turn, carry):
        shard = (turn + first_unit // 2) % SIDE
        kept = []
        for v in range(2):
            t = 2 * shard + v
            for h in range(2):
                chunk = 2 * t + h
                a, b = axes(h)
                rows = gain_rows(t, h)
                unit = (wide(both[0, chunk]) - mean) * inv_scale
                d_normed = wide(both[1, chunk])
                grad = inv_scale * (rows * d_normed - mean_scaled - unit * mean_product)
                value = jnp.where(section == 0, grad, unit * rows)
                values[chunk, b, a] = narrow(value)
                gather_values(t, h, 0).start()
                gather_values(t, h, 1).start()
                kept.append(value)
                product = d_normed * unit
                for start, rows in (
                    (lower_start(t, h), slice(0, OWN)),
                    (upper_start(t, h), slice(OWN, TALL)),
                ):
                    own_grad[:, pl.ds(start, WIDE)] = narrow(grad[rows])
                    gain_own[0, :, pl.ds(start, WIDE)] = jnp.sum(product[rows], axis=0, keepdims=True)
        for target, rows in ((shard, slice(0, OWN)), (GROUPS - 1 - shard, slice(OWN, TALL))):
            for e, (first, second) in enumerate(((0, 2), (1, 3), (2, 3))):
                exchange[target, e] = narrow(stacked(kept[first][rows], kept[second][rows]))
                wanted = target // SIDE != z // 2 if e < 2 else target // 2 == next_plane

                @pl.when(wanted)
                def _():
                    exchanged(target, e).start()
        return carry

    lax.fori_loop(0, SIDE, write, 0)


    def near_copy(t, upper, target, slot):
        return remote(
            tokens.at[t, upper],
            from_near.at[slot],
            near_send.at[0],
            near_recv.at[slot],
            {"grp": target},
        )

    def split_blocks(store, chunk, h, put):
        for i in range(0, SIDE * SIDE, 2):
            pair = []
            for at in (i, i + 1):
                a, b = (at // SIDE, at % SIDE) if h == 0 else (at % SIDE, at // SIDE)
                pair.append(wide(store[chunk, b, a]))
            put(0, slice(OWN * i, OWN * (i + 2)), narrow(stacked(pair[0][:OWN], pair[1][:OWN])))
            put(1, slice(OWN * i, OWN * (i + 2)), narrow(stacked(pair[0][OWN:], pair[1][OWN:])))

    def add_grads(start, transposed_heads, token_rows):
        cols = pl.ds(start, token_rows.shape[1])
        grads_t[:, cols] += jnp.dot(
            transposed_heads, token_rows, preferred_element_type=jnp.float32
        )

    def store_grads(block):
        return pltpu.make_async_copy(
            grads.at[block * WIDE : (block + 1) * WIDE],
            grads_out.at[block * WIDE : (block + 1) * WIDE],
            output_sem.at[3 + block],
        )

    def finish_grads(blocks):
        for block in blocks:
            cols = slice(block * WIDE, (block + 1) * WIDE)
            grads[cols] = grad_scale * grads_t[:, cols].T
            store_grads(block).start()

    def use_values(t):
        for h in range(2):

            def put(upper, rows, block):
                tokens[t, upper, rows, h * WIDE : (h + 1) * WIDE] = block

            split_blocks(values, 2 * t + h, h, put)
        for upper, target in enumerate((t // 2, GROUPS - 1 - t // 2)):
            to_next = jnp.logical_and(target // 2 == next_plane, t % 2 == 0)
            for slot, wanted in ((t % 2, target == sibling_group), (2 + core, to_next)):

                @pl.when(wanted)
                def _():
                    near_copy(t, upper, target, slot).start()

        total = heads_total[...]
        for upper, start in enumerate((lower_start(t), upper_start(t))):
            total = total + lax.dot_general(
                tokens[t, upper], weight_buf[:, pl.ds(start, UNIT_WIDE)],
                (((1,), (1,)), ((), ())), preferred_element_type=jnp.float32,
            )
        heads_total[...] = total
        for upper, target in enumerate((t // 2, GROUPS - 1 - t // 2)):

            @pl.when(target == group)
            def _():
                add_grads(pl.multiple_of((t % 2) * UNIT_WIDE, UNIT_WIDE), heads_t[...], tokens[t, upper])

    def use_columns(p):
        last = p // (FAR_UNITS - 1)
        plane = (1 - last) * (2 * (1 - z // 2) + p // 2) + last * next_plane
        for h in range(2):

            def put(side, rows, block):
                column_tokens[h, rows, side * WIDE : (side + 1) * WIDE] = block

            split_blocks(columns, 2 * p + h, h, put)
        slot = plane_slot(plane, z)

        @pl.when(jnp.logical_and(p % 2 == 0, last == 0))
        def _():
            heads_arrived(slot + 1 - core)

        total = jnp.dot(
            heads_all[slot], column_tokens[0], preferred_element_type=jnp.float32
        ) + jnp.dot(heads_all[slot + 1], column_tokens[1], preferred_element_type=jnp.float32)
        for side in range(2):
            start = (1 - last) * (side * UNIT_WIDE + (p % 2) * WIDE) + last * (UNIT_WIDE + side * WIDE)
            cols = pl.ds(pl.multiple_of(start, WIDE), WIDE)
            grads_t[:, cols] += total[:, side * WIDE : (side + 1) * WIDE]

    def use_near(slot, heads_slot, start):
        wait_arrived(from_near.at[slot], near_recv.at[slot])
        add_grads(start, heads_all[heads_slot], from_near[slot])

    gain_partners = [
        {"tp": x * SIDE + y + 1 - 2 * (y % 2)},
        {"tp": x * SIDE + SIDE - 1 - y},
        {"tp": (x + 1 - 2 * (x % 2)) * SIDE + y},
        {"tp": (SIDE - 1 - x) * SIDE + y},
        sibling,
        {"grp": 2 * next_plane + core},
        {"grp": 2 * (SIDE - 1 - z) + core},
    ]

    def gain_copy(step):
        return remote(
            gain_own.at[step], gain_got.at[step], gain_send.at[step], gain_recv.at[step], gain_partners[step]
        )

    own_grad_store, heads_store, gain_store = [
        pltpu.make_async_copy(source, target, output_sem.at[at])
        for at, (source, target) in enumerate(
            ((own_grad, grad_out), (heads_done, heads_out), (gain_done, gain_out))
        )
    ]

    near_heads = plane_slot(next_plane, z)

    def value_unit(q):
        return (q + first_unit) % UNITS

    def gather_stage(q, stage):
        def pass_on(gather, recvs, p):
            wait_arrived(gather_sizes[stage], recvs.at[p, stage])
            if stage < 3:
                for h in range(2):
                    gather(p, h, 2 * stage + 2).start()
                    gather(p, h, 2 * stage + 3).start()

        @pl.when(within(q, UNITS))
        def _():
            pass_on(gather_values, value_recv, value_unit(q))

        @pl.when(within(q - UNITS, FAR_UNITS))
        def _():
            pass_on(gather_columns, column_recv, q - UNITS)

    def gather_turn(n, carry):
        @pl.when(n == 5)
        def _():
            pass_heads()

        for step in range(GAIN_STEPS + 1):

            @pl.when(n == step + 1)
            def _():
                if step > 0:
                    gain_copy(step - 1).wait_recv()
                    gain_own[step] = gain_own[step - 1] + gain_got[step - 1]
                if step < GAIN_STEPS:
                    gain_copy(step).start()
                else:
                    gain_done[...] = gain_own[GAIN_STEPS] * grad_scale
                    gain_store.start()

        @pl.when(within(n + 1 - UNITS, FAR_UNITS))
        def _():
            p = n + 1 - UNITS
            wait_arrived(gather_sizes[1], exchange_recv.at[p])
            for h in range(2):
                gather_columns(p, h, 0).start()
                gather_columns(p, h, 1).start()

        @pl.when(n == UNITS + FAR_UNITS + 4)
        def _():
            finish_grads((0, 1))

        gather_stage(n, 0)
        gather_stage(n - 4, 2)
        gather_stage(n - 2, 1)
        gather_stage(n - 5, 3)
        done = n - 5

        @pl.when(within(done, UNITS))
        def _():
            use_values(value_unit(done))

        @pl.when(done == UNITS)
        def _():
            heads_done[...] = narrow(heads_total[...])
            heads_store.start()
            heads_arrived(SLOTS - 1)
            use_near(0, SLOTS - 1, 0)
            use_near(1, SLOTS - 1, UNIT_WIDE)
            heads_arrived(near_heads + 1 - core)

        @pl.when(done == UNITS + 2)
        def _():
            for k in range(2):
                use_near(2 + k, near_heads + k, 0)

        @pl.when(within(done - UNITS, FAR_UNITS))
        def _():
            use_columns(done - UNITS)

        return carry

    own_grad_store.start()
    each_relay((2,), pass_relay)
    lax.fori_loop(0, UNITS + FAR_UNITS + 5, gather_turn, 0)
    finish_grads((2, 3))

    def reduce_sent(u, carry):
        wait_sent(part.at[0:2], send_sem.at[u])
        wait_sent(values.at[0:5, 0:3, 0:2], value_send.at[u])
        return carry

    def columns_sent(p, carry):
        wait_sent(values.at[0:5, 0:3, 0:2], column_send.at[p])
        return carry

    lax.fori_loop(0, UNITS, reduce_sent, 0)
    lax.fori_loop(0, FAR_UNITS, columns_sent, 0)
    wait_sent(exchange.at[0:5, 0:2], exchange_send.at[0])
    wait_sent(tokens.at[0:2], near_send.at[0])
    each_relay((0, 1, 2), lambda relay, held: relay.wait_send())
    for j in range(SIDE - 1):
        passed_heads(j).wait_send()
    sibling_heads().wait_send()
    for step in range(GAIN_STEPS):
        gain_copy(step).wait_send()
    for store in [own_grad_store, heads_store, gain_store] + [store_grads(i) for i in range(4)]:
        store.wait()


def deliver_kernel(*refs):
    results, outputs, held = refs[:4], refs[4:8], refs[8:12]
    load_sem, store_sem = refs[12:]
    loads = [pltpu.make_async_copy(results[at], held[at], load_sem.at[at]) for at in range(4)]
    stores = [pltpu.make_async_copy(held[at], outputs[at], store_sem.at[at]) for at in range(4)]
    for load in loads:
        load.start()
    for load, store in zip(loads, stores):
        load.wait()
        store.start()
    for store in stores:
        store.wait()


def delivered(results):
    hbm = pl.BlockSpec(memory_space=pl.ANY)
    return pl.pallas_call(
        deliver_kernel,
        out_shape=tuple(jax.ShapeDtypeStruct(result.shape, result.dtype) for result in results),
        in_specs=[hbm] * 4,
        out_specs=(hbm,) * 4,
        scratch_shapes=[pltpu.VMEM(result.shape, result.dtype) for result in results]
        + [pltpu.SemaphoreType.DMA((4,))] * 2,
        name="deliver",
    )(*results)


def fused(heads, weights, residual, gain):
    hbm = pl.BlockSpec(memory_space=pl.ANY)
    bf16, f32 = jnp.bfloat16, jnp.float32
    rows_dev, depth = heads.shape
    owned = weights.shape[1] // GROUPS
    dma = pltpu.SemaphoreType.DMA
    return pl.pallas_call(
        boundary_kernel,
        out_shape=(
            jax.ShapeDtypeStruct(heads.shape, bf16),
            jax.ShapeDtypeStruct((owned, depth), f32),
            jax.ShapeDtypeStruct(residual.shape, bf16),
            jax.ShapeDtypeStruct(gain.shape, f32),
        ),
        in_specs=[hbm] * 4,
        out_specs=(hbm,) * 4,
        scratch_shapes=[
            pltpu.VMEM(heads.shape, bf16),
            pltpu.VMEM(residual.shape, bf16),
            pltpu.VMEM(gain.shape, f32),
            pltpu.VMEM(heads.shape, bf16),
            pltpu.VMEM((owned, depth), f32),
            pltpu.VMEM(residual.shape, bf16),
            pltpu.VMEM(gain.shape, f32),
            pltpu.VMEM((depth, rows_dev), bf16),
            pltpu.VMEM((depth, owned), f32),
            pltpu.VMEM(weights.shape, bf16),
            pltpu.VMEM((CHUNKS, SIDE, SIDE, TALL, WIDE), bf16),
            pltpu.VMEM((CHUNKS, 2, SIDE, TALL, HALF), bf16),
            pltpu.VMEM((CHUNKS, 2, SIDE, TALL, WIDE), bf16),
            pltpu.VMEM((CHUNKS, 2, TALL, HALF), bf16),
            pltpu.VMEM((CHUNKS, 2, TALL, WIDE), bf16),
            pltpu.VMEM((2, CHUNKS, TALL, WIDE), bf16),
            pltpu.VMEM((CHUNKS, SIDE, SIDE, TALL, WIDE), bf16),
            pltpu.VMEM((FAR_CHUNKS, SIDE, SIDE, TALL, WIDE), bf16),
            pltpu.VMEM((GROUPS, 3, TALL, WIDE), bf16),
            pltpu.VMEM((UNITS, 2, rows_dev, UNIT_WIDE), bf16),
            pltpu.VMEM((2, rows_dev, UNIT_WIDE), bf16),
            pltpu.VMEM((4, rows_dev, UNIT_WIDE), bf16),
            pltpu.VMEM((SLOTS, depth, rows_dev), bf16),
            pltpu.VMEM((rows_dev, depth), f32),
            pltpu.VMEM((GAIN_STEPS + 1,) + gain.shape, f32),
            pltpu.VMEM((GAIN_STEPS,) + gain.shape, f32),
            dma((3,)),
            dma((7,)),
            dma((UNITS, 2)),
            dma((UNITS,)),
            dma((UNITS, 5)),
            dma((UNITS,)),
            dma((UNITS, 4)),
            dma((FAR_UNITS,)),
            dma((FAR_UNITS, 4)),
            dma((1,)),
            dma((FAR_UNITS,)),
            dma((SLOTS + 6,)),
            dma((SLOTS,)),
            dma((1,)),
            dma((4,)),
            dma((GAIN_STEPS,)),
            dma((GAIN_STEPS,)),
        ],
        compiler_params=pltpu.CompilerParams(
            collective_id=0, has_side_effects=True, vmem_limit_bytes=62 * 1024 * 1024
        ),
        name="boundary",
    )(heads, weights, residual, gain)


def per_device(heads_in, weights, residual, norm_gain):
    heads_out, weight_grad, boundary_grad, gain_grad = delivered(
        fused(heads_in[0], weights[0], residual, norm_gain[None])
    )
    return (heads_out[None], weight_grad[None], boundary_grad, gain_grad[0])


def solution(mesh):
    placed = (P("section", "grp", "tp"), P("section", "tp", None), P(("grp", "tp"), None), P())
    return jax.shard_map(
        per_device,
        mesh=mesh,
        in_specs=placed,
        out_specs=(
            P("section", "grp", "tp"),
            P("section", "grp", "tp"),
            P(("grp", "tp"), None),
            P(),
        ),
        check_vma=False,
    )
```

profile of v0, /device:TPU:2, one launch (start us, length us, event | category | flops | bytes accessed | tf_op | source)
XLA Modules:
  0.0 129.1 jit_solution(5831561918587847155)
XLA Ops:
  0.6 125.2 %boundary.1 = (bf16[384,512]{1,0:T(8,128)(2,1)}, f32[1024,512]{1,0:T(8,128)}, bf16[24,8192]{1,0:T(8,128)(2,1)}, f32[1,8192]{1,0:T(1,128)}) custom-call(bf16[384,512]{1,0:T(8,128)(2,1)} %bitcast.7, bf16[512,8192]{1,0:T(8,128)(2,1)} %bitcast.6, bf16[24,8192]{1,0:T(8,128)(2,1)} %residual_in.1, f32[1,8192]{1,0:T(1,128)} %bitcast.8), custom_call_target="tpu_custom_call" | custom-call | tf_op jit(solution)/shard_map/boundary/pallas_call | solution.py:704
  125.8 3.2 %deliver.1 = (bf16[384,512]{1,0:T(8,128)(2,1)}, f32[1024,512]{1,0:T(8,128)}, bf16[24,8192]{1,0:T(8,128)(2,1)}, f32[1,8192]{1,0:T(1,128)}) custom-call(bf16[384,512]{1,0:T(8,128)(2,1)} %get-tuple-element.12.refs_0_, f32[1024,512]{1,0:T(8,128)} %get-tuple-element.13.refs_1_, bf16[24,8192]{1,0:T(8,128)(2,1)} %get-tuple-element.14.refs_2_, ...), custom_call_target="tpu_custom_call" | custom-call | tf_op jit(solution)/shard_map/deliver/pallas_call | solution.py:687
where the time goes:
time: 129 us
  Pallas kernels  128 us (99%)
    pallas_call x1, Pallas kernels, fused(): pl.pallas_call(boundary_kernel, out_shape=(jax.ShapeDtypeStruct(heads.sha...  125 us
    pallas_call x1, Pallas kernels, delivered(): pl.pallas_call(deliver_kernel, out_shape=tuple((jax.ShapeDtypeStruct(resu...  3.24 us

commit v1 on v0

--- a/solution.py
+++ b/solution.py
@@ -15,9 +15,9 @@
 UNITS = 8
 FAR_UNITS = 5
 CHUNKS = 2 * UNITS
-FAR_CHUNKS = 2 * FAR_UNITS
+ALL_UNITS = UNITS + FAR_UNITS
+GATHER_GROUPS = ((0, 2), (2, UNITS - 2), (UNITS, FAR_UNITS))
 WIDE = 256
-HALF = WIDE // 2
 UNIT_WIDE = 2 * WIDE
 SHARD = 2 * UNIT_WIDE
 OWN = 24
@@ -82,8 +82,8 @@
     heads_in, weights, residual_in, gain_in, heads_out, grads_out, grad_out, gain_out,
     heads, residual, gain, heads_done, grads, own_grad, gain_done,
     heads_t, grads_t, weight_buf, part, from1, from2, from3, from4, both,
-    values, columns, exchange, tokens, column_tokens, from_near, heads_all, heads_total, gain_own, gain_got,
-    input_sem, output_sem, weight_sem, send_sem, recv_sem, value_send, value_recv, column_send, column_recv,
+    values, exchange, tokens, column_tokens, from_near, heads_all, heads_total, gain_own, gain_got,
+    input_sem, output_sem, weight_sem, send_sem, recv_sem, group_send, group_recv, unit_send, unit_recv,
     exchange_send, exchange_recv, heads_send, heads_recv, near_send, near_recv, gain_send, gain_recv,
 ):
     tp = lax.axis_index("tp")
@@ -206,20 +206,20 @@
         a, b = axes(h)
         right, left = (a + 1) % SIDE, (a + 3) % SIDE
         up, down = (b + 1) % SIDE, (b + 3) % SIDE
-        low, high = pl.ds(0, HALF), pl.ds(HALF, HALF)
         far_a, far_b = (a + 2) % SIDE, (b + 2) % SIDE
+        odd = u % 2
+        way_a, way_b = (a + 1 + 2 * odd) % SIDE, (b + 1 + 2 * odd) % SIDE
         source, target, device = [
-            lambda: (part.at[chunk, far_a, :, :, low], from1.at[chunk, 0], plane_device(h, right, b)),
-            lambda: (part.at[chunk, far_a, :, :, high], from1.at[chunk, 1], plane_device(h, left, b)),
+            lambda: (part.at[chunk, far_a], from1.at[chunk], plane_device(h, way_a, b)),
             lambda: (part.at[chunk, right], from2.at[chunk, 0], plane_device(h, right, b)),
             lambda: (part.at[chunk, left], from2.at[chunk, 1], plane_device(h, left, b)),
-            lambda: (part.at[chunk, a, far_b, :, low], from3.at[chunk, 0], plane_device(h, a, up)),
-            lambda: (part.at[chunk, a, far_b, :, high], from3.at[chunk, 1], plane_device(h, a, down)),
+            lambda: (part.at[chunk, a, far_b], from3.at[chunk], plane_device(h, a, way_b)),
             lambda: (part.at[chunk, a, up], from4.at[chunk, 0], plane_device(h, a, up)),
             lambda: (part.at[chunk, a, down], from4.at[chunk, 1], plane_device(h, a, down)),
             lambda: (both.at[section, chunk], both.at[section, chunk], other),
         ][step]()
-        return remote(source, target, send_sem.at[u], recv_sem.at[u, step // 2], device)
+        stage = (0, 1, 1, 2, 3, 3, 4)[step]
+        return remote(source, target, send_sem.at[u], recv_sem.at[u, stage], device)
 
     reduce_sizes = [
         part.at[0, 0:2], part.at[0], part.at[0, 0, 0:2], part.at[0, 0], part.at[0, 0, 0:2]
@@ -245,22 +245,15 @@
                 a, b = (i // SIDE, i % SIDE) if h == 0 else (i % SIDE, i // SIDE)
                 part[2 * u + h, a, b] = narrow(stacked(lower[rows, cols], upper[rows, cols]))
             copy(u, h, 0).start()
-            copy(u, h, 1).start()
 
     def near_first(u):
         arrive(u, 0)
         for h in range(2):
             chunk = 2 * u + h
-            a, b = axes(h)
-            right, left = (a + 1) % SIDE, (a + 3) % SIDE
-            part[chunk, right, :, :, :HALF] = narrow(
-                wide(part[chunk, right, :, :, :HALF]) + wide(from1[chunk, 0])
-            )
+            near = (axes(h)[0] + 1 + 2 * (u % 2)) % SIDE
+            part[chunk, near] = narrow(wide(part[chunk, near]) + wide(from1[chunk]))
+            copy(u, h, 1).start()
             copy(u, h, 2).start()
-            part[chunk, left, :, :, HALF:] = narrow(
-                wide(part[chunk, left, :, :, HALF:]) + wide(from1[chunk, 1])
-            )
-            copy(u, h, 3).start()
 
     def far_second(u):
         arrive(u, 1)
@@ -270,23 +263,17 @@
             part[chunk, a] = narrow(
                 wide(part[chunk, a]) + (wide(from2[chunk, 0]) + wide(from2[chunk, 1]))
             )
+            copy(u, h, 3).start()
+
+    def near_second(u):
+        arrive(u, 2)
+        for h in range(2):
+            chunk = 2 * u + h
+            a, b = axes(h)
+            near = (b + 1 + 2 * (u % 2)) % SIDE
+            part[chunk, a, near] = narrow(wide(part[chunk, a, near]) + wide(from3[chunk]))
             copy(u, h, 4).start()
             copy(u, h, 5).start()
-
-    def near_second(u):
-        arrive(u, 2)
-        for h in range(2):
-            chunk = 2 * u + h
-            a, b = axes(h)
-            up, down = (b + 1) % SIDE, (b + 3) % SIDE
-            part[chunk, a, up, :, :HALF] = narrow(
-                wide(part[chunk, a, up, :, :HALF]) + wide(from3[chunk, 0])
-            )
-            copy(u, h, 6).start()
-            part[chunk, a, down, :, HALF:] = narrow(
-                wide(part[chunk, a, down, :, HALF:]) + wide(from3[chunk, 1])
-            )
-            copy(u, h, 7).start()
 
     def finish(u):
         arrive(u, 3)
@@ -300,7 +287,7 @@
             )
             total = total + jnp.where(section == 0, rows, 0.0)
             both[section, chunk] = narrow(total)
-            copy(u, h, 8).start()
+            copy(u, h, 6).start()
 
     def within(value, count):
         return jnp.logical_and(value >= 0, value < count)
@@ -331,42 +318,50 @@
     grads_t[...] = jnp.zeros_like(grads_t)
 
 
-    def gather_of(store, sends, recvs):
-        half = store.shape[-1] // 2
-
-        def gather(p, h, step):
-            chunk = 2 * p + h
-            a, b = axes(h)
-            right, left = (a + 1) % SIDE, (a + 3) % SIDE
-            up, down = (b + 1) % SIDE, (b + 3) % SIDE
-            low, high = pl.ds(0, half), pl.ds(half, half)
-            block, device = [
-                lambda: (store.at[chunk, b, a], plane_device(h, right, b)),
-                lambda: (store.at[chunk, b, a], plane_device(h, left, b)),
-                lambda: (store.at[chunk, b, left, :, low], plane_device(h, right, b)),
-                lambda: (store.at[chunk, b, right, :, high], plane_device(h, left, b)),
-                lambda: (store.at[chunk, b], plane_device(h, a, up)),
-                lambda: (store.at[chunk, b], plane_device(h, a, down)),
-                lambda: (store.at[chunk, down, :, :, low], plane_device(h, a, up)),
-                lambda: (store.at[chunk, up, :, :, high], plane_device(h, a, down)),
-            ][step]()
-            return remote(block, block, sends.at[p], recvs.at[p, step // 2], device)
-
-        return gather
-
-    gather_values = gather_of(values, value_send, value_recv)
-    gather_columns = gather_of(columns, column_send, column_recv)
-
-    gather_sizes = [values.at[0, 0], values.at[0, 0, 0:2], values.at[0], values.at[0, 0:2]]
+    def gather_first(group, h, step):
+        first, count = GATHER_GROUPS[group]
+        a, b = axes(h)
+        right, left = (a + 1) % SIDE, (a + 3) % SIDE
+        half = (count + 1) // 2
+        block, way = [
+            lambda: (values.at[h, first : first + count, b, a], right),
+            lambda: (values.at[h, first : first + count, b, a], left),
+            lambda: (values.at[h, first : first + half, b, left], right),
+            lambda: (values.at[h, first + half : first + count, b, right], left),
+        ][step]()
+        sems = group_send.at[group], group_recv.at[group, step // 2]
+        return remote(block, block, *sems, plane_device(h, way, b))
+
+    def gather_second(q, h, step):
+        a, b = axes(h)
+        up, down = (b + 1) % SIDE, (b + 3) % SIDE
+        odd = q % 2
+        block, way = [
+            lambda: (values.at[h, q, b], up),
+            lambda: (values.at[h, q, b], down),
+            lambda: (values.at[h, q, (b + 3 + 2 * odd) % SIDE], (b + 1 + 2 * odd) % SIDE),
+        ][step]()
+        sems = unit_send.at[q], unit_recv.at[q, step // 2]
+        return remote(block, block, *sems, plane_device(h, a, way))
+
+    def start_group(group, steps):
+        for h in range(2):
+            for step in steps:
+                gather_first(group, h, step).start()
+
+    def start_unit(q, steps):
+        for h in range(2):
+            for step in steps:
+                gather_second(q, h, step).start()
 
     def exchanged(target, e):
         unit = 2 * (z % 2) + e if e < 2 else FAR_UNITS - 1
         a, b = x + core * (y - x), y + core * (x - y)
         return remote(
             exchange.at[target, e],
-            columns.at[2 * unit + core, b, a],
+            values.at[core, UNITS + unit, b, a],
             exchange_send.at[0],
-            exchange_recv.at[unit],
+            exchange_recv.at[0],
             {"grp": target},
         )
 
@@ -421,9 +416,7 @@
                 d_normed = wide(both[1, chunk])
                 grad = inv_scale * (rows * d_normed - mean_scaled - unit * mean_product)
                 value = jnp.where(section == 0, grad, unit * rows)
-                values[chunk, b, a] = narrow(value)
-                gather_values(t, h, 0).start()
-                gather_values(t, h, 1).start()
+                values[h, 2 * turn + v, b, a] = narrow(value)
                 kept.append(value)
                 product = d_normed * unit
                 for start, rows in (
@@ -440,9 +433,15 @@
                 @pl.when(wanted)
                 def _():
                     exchanged(target, e).start()
+
+        @pl.when(turn == 0)
+        def _():
+            start_group(0, (0, 1))
+
         return carry
 
     lax.fori_loop(0, SIDE, write, 0)
+    start_group(1, (0, 1))
 
 
     def near_copy(t, upper, target, slot):
@@ -454,12 +453,12 @@
             {"grp": target},
         )
 
-    def split_blocks(store, chunk, h, put):
+    def split_blocks(q, h, put):
         for i in range(0, SIDE * SIDE, 2):
             pair = []
             for at in (i, i + 1):
                 a, b = (at // SIDE, at % SIDE) if h == 0 else (at % SIDE, at // SIDE)
-                pair.append(wide(store[chunk, b, a]))
+                pair.append(wide(values[h, q, b, a]))
             put(0, slice(OWN * i, OWN * (i + 2)), narrow(stacked(pair[0][:OWN], pair[1][:OWN])))
             put(1, slice(OWN * i, OWN * (i + 2)), narrow(stacked(pair[0][OWN:], pair[1][OWN:])))
 
@@ -482,13 +481,14 @@
             grads[cols] = grad_scale * grads_t[:, cols].T
             store_grads(block).start()
 
-    def use_values(t):
+    def use_values(q):
+        t = (q + first_unit) % UNITS
         for h in range(2):
 
             def put(upper, rows, block):
                 tokens[t, upper, rows, h * WIDE : (h + 1) * WIDE] = block
 
-            split_blocks(values, 2 * t + h, h, put)
+            split_blocks(q, h, put)
         for upper, target in enumerate((t // 2, GROUPS - 1 - t // 2)):
             to_next = jnp.logical_and(target // 2 == next_plane, t % 2 == 0)
             for slot, wanted in ((t % 2, target == sibling_group), (2 + core, to_next)):
@@ -518,7 +518,7 @@
             def put(side, rows, block):
                 column_tokens[h, rows, side * WIDE : (side + 1) * WIDE] = block
 
-            split_blocks(columns, 2 * p + h, h, put)
+            split_blocks(UNITS + p, h, put)
         slot = plane_slot(plane, z)
 
         @pl.when(jnp.logical_and(p % 2 == 0, last == 0))
@@ -560,25 +560,6 @@
     ]
 
     near_heads = plane_slot(next_plane, z)
-
-    def value_unit(q):
-        return (q + first_unit) % UNITS
-
-    def gather_stage(q, stage):
-        def pass_on(gather, recvs, p):
-            wait_arrived(gather_sizes[stage], recvs.at[p, stage])
-            if stage < 3:
-                for h in range(2):
-                    gather(p, h, 2 * stage + 2).start()
-                    gather(p, h, 2 * stage + 3).start()
-
-        @pl.when(within(q, UNITS))
-        def _():
-            pass_on(gather_values, value_recv, value_unit(q))
-
-        @pl.when(within(q - UNITS, FAR_UNITS))
-        def _():
-            pass_on(gather_columns, column_recv, q - UNITS)
 
     def gather_turn(n, carry):
         @pl.when(n == 5)
@@ -598,27 +579,47 @@
                     gain_done[...] = gain_own[GAIN_STEPS] * grad_scale
                     gain_store.start()
 
-        @pl.when(within(n + 1 - UNITS, FAR_UNITS))
-        def _():
-            p = n + 1 - UNITS
-            wait_arrived(gather_sizes[1], exchange_recv.at[p])
-            for h in range(2):
-                gather_columns(p, h, 0).start()
-                gather_columns(p, h, 1).start()
-
-        @pl.when(n == UNITS + FAR_UNITS + 4)
+        @pl.when(n == 3)
+        def _():
+            wait_arrived(values.at[0:2, 0:FAR_UNITS, 0, 0], exchange_recv.at[0])
+            start_group(2, (0, 1))
+
+        for group, at in enumerate((0, 1, 5)):
+            count = GATHER_GROUPS[group][1]
+
+            @pl.when(n == at)
+            def _():
+                wait_arrived(values.at[0:2, 0:count, 0, 0:2], group_recv.at[group, 0])
+                start_group(group, (2, 3))
+
+        @pl.when(within(n - 2, ALL_UNITS))
+        def _():
+            wait_arrived(values.at[0:2, 0:2, 0], unit_recv.at[n - 2, 0])
+            start_unit(n - 2, (2,))
+
+        for group, (first, count) in enumerate(GATHER_GROUPS):
+
+            @pl.when(n == first)
+            def _():
+                wait_arrived(values.at[0:2, 0:count, 0, 0], group_recv.at[group, 1])
+
+        @pl.when(n < ALL_UNITS)
+        def _():
+            start_unit(n, (0, 1))
+
+        done = n - 3
+
+        @pl.when(done == ALL_UNITS - 1)
         def _():
             finish_grads((0, 1))
 
-        gather_stage(n, 0)
-        gather_stage(n - 4, 2)
-        gather_stage(n - 2, 1)
-        gather_stage(n - 5, 3)
-        done = n - 5
+        @pl.when(within(done, ALL_UNITS))
+        def _():
+            wait_arrived(values.at[0:2, 0, 0], unit_recv.at[done, 1])
 
         @pl.when(within(done, UNITS))
         def _():
-            use_values(value_unit(done))
+            use_values(done)
 
         @pl.when(done == UNITS)
         def _():
@@ -642,20 +643,21 @@
 
     own_grad_store.start()
     each_relay((2,), pass_relay)
-    lax.fori_loop(0, UNITS + FAR_UNITS + 5, gather_turn, 0)
+    lax.fori_loop(0, ALL_UNITS + 3, gather_turn, 0)
     finish_grads((2, 3))
 
     def reduce_sent(u, carry):
         wait_sent(part.at[0:2], send_sem.at[u])
-        wait_sent(values.at[0:5, 0:3, 0:2], value_send.at[u])
         return carry
 
-    def columns_sent(p, carry):
-        wait_sent(values.at[0:5, 0:3, 0:2], column_send.at[p])
+    def gather_sent(q, carry):
+        wait_sent(values.at[0:2, 0:3, 0], unit_send.at[q])
         return carry
 
     lax.fori_loop(0, UNITS, reduce_sent, 0)
-    lax.fori_loop(0, FAR_UNITS, columns_sent, 0)
+    lax.fori_loop(0, ALL_UNITS, gather_sent, 0)
+    for group, (first, count) in enumerate(GATHER_GROUPS):
+        wait_sent(values.at[0:2, 0:count, 0, 0:3], group_send.at[group])
     wait_sent(exchange.at[0:5, 0:2], exchange_send.at[0])
     wait_sent(tokens.at[0:2], near_send.at[0])
     each_relay((0, 1, 2), lambda relay, held: relay.wait_send())
@@ -723,13 +725,12 @@
             pltpu.VMEM((depth, owned), f32),
             pltpu.VMEM(weights.shape, bf16),
             pltpu.VMEM((CHUNKS, SIDE, SIDE, TALL, WIDE), bf16),
-            pltpu.VMEM((CHUNKS, 2, SIDE, TALL, HALF), bf16),
+            pltpu.VMEM((CHUNKS, SIDE, TALL, WIDE), bf16),
             pltpu.VMEM((CHUNKS, 2, SIDE, TALL, WIDE), bf16),
-            pltpu.VMEM((CHUNKS, 2, TALL, HALF), bf16),
+            pltpu.VMEM((CHUNKS, TALL, WIDE), bf16),
             pltpu.VMEM((CHUNKS, 2, TALL, WIDE), bf16),
             pltpu.VMEM((2, CHUNKS, TALL, WIDE), bf16),
-            pltpu.VMEM((CHUNKS, SIDE, SIDE, TALL, WIDE), bf16),
-            pltpu.VMEM((FAR_CHUNKS, SIDE, SIDE, TALL, WIDE), bf16),
+            pltpu.VMEM((2, ALL_UNITS, SIDE, SIDE, TALL, WIDE), bf16),
             pltpu.VMEM((GROUPS, 3, TALL, WIDE), bf16),
             pltpu.VMEM((UNITS, 2, rows_dev, UNIT_WIDE), bf16),
             pltpu.VMEM((2, rows_dev, UNIT_WIDE), bf16),
@@ -743,12 +744,12 @@
             dma((UNITS, 2)),
             dma((UNITS,)),
             dma((UNITS, 5)),
-            dma((UNITS,)),
-            dma((UNITS, 4)),
-            dma((FAR_UNITS,)),
-            dma((FAR_UNITS, 4)),
+            dma((len(GATHER_GROUPS),)),
+            dma((len(GATHER_GROUPS), 2)),
+            dma((ALL_UNITS,)),
+            dma((ALL_UNITS, 2)),
             dma((1,)),
-            dma((FAR_UNITS,)),
+            dma((1,)),
             dma((SLOTS + 6,)),
             dma((SLOTS,)),
             dma((1,)),

time: 129 us -> 132 us (1.023)
  Pallas kernels: 128 us -> 131 us
    pallas_call x1, Pallas kernels: 125 us -> 128 us  [fused(): pl.pallas_call(boundary_kernel, out_shape=(jax.ShapeDtypeStruct(heads.sha...]
where the time goes in v1:
time: 132 us
  Pallas kernels  131 us (99%)
    pallas_call x1, Pallas kernels, fused(): pl.pallas_call(boundary_kernel, out_shape=(jax.ShapeDtypeStruct(heads.sha...  128 us
    pallas_call x1, Pallas kernels, delivered(): pl.pallas_call(deliver_kernel, out_shape=tuple((jax.ShapeDtypeStruct(resu...  3.24 us

profile of v1, /device:TPU:2, one launch (start us, length us, event | category | flops | bytes accessed | tf_op | source)
XLA Modules:
  0.0 131.8 jit_solution(17235338181571528030)
XLA Ops:
  0.6 127.9 %boundary.1 = (bf16[384,512]{1,0:T(8,128)(2,1)}, f32[1024,512]{1,0:T(8,128)}, bf16[24,8192]{1,0:T(8,128)(2,1)}, f32[1,8192]{1,0:T(1,128)}) custom-call(bf16[384,512]{1,0:T(8,128)(2,1)} %bitcast.7, bf16[512,8192]{1,0:T(8,128)(2,1)} %bitcast.6, bf16[24,8192]{1,0:T(8,128)(2,1)} %residual_in.1, f32[1,8192]{1,0:T(1,128)} %bitcast.8), custom_call_target="tpu_custom_call" | custom-call | tf_op jit(solution)/shard_map/boundary/pallas_call | solution.py:706
  128.6 3.2 %deliver.1 = (bf16[384,512]{1,0:T(8,128)(2,1)}, f32[1024,512]{1,0:T(8,128)}, bf16[24,8192]{1,0:T(8,128)(2,1)}, f32[1,8192]{1,0:T(1,128)}) custom-call(bf16[384,512]{1,0:T(8,128)(2,1)} %get-tuple-element.12.refs_0_, f32[1024,512]{1,0:T(8,128)} %get-tuple-element.13.refs_1_, bf16[24,8192]{1,0:T(8,128)(2,1)} %get-tuple-element.14.refs_2_, ...), custom_call_target="tpu_custom_call" | custom-call | tf_op jit(solution)/shard_map/deliver/pallas_call | solution.py:689

commit v2 on v0

--- a/solution.py
+++ b/solution.py
@@ -247,6 +247,11 @@
             copy(u, h, 0).start()
             copy(u, h, 1).start()
 
+    def transpose_weights(u):
+        for start in (lower_start(u), upper_start(u)):
+            cols = pl.ds(start, UNIT_WIDE)
+            weight_buf[:, cols] = weight_buf[:, cols].T
+
     def near_first(u):
         arrive(u, 0)
         for h in range(2):
@@ -306,6 +311,7 @@
         return jnp.logical_and(value >= 0, value < count)
 
     stages = (multiply, near_first, far_second, near_second, finish)
+    TRANSPOSE_TURN = 4
 
     def reduce_turn(n, carry):
         for late, stage in enumerate(stages):
@@ -313,6 +319,10 @@
             @pl.when(within(n - late, UNITS))
             def _():
                 stage(n - late)
+
+        @pl.when(within(n - TRANSPOSE_TURN, UNITS))
+        def _():
+            transpose_weights(n - TRANSPOSE_TURN)
 
         @pl.when(n == 1)
         def _():
@@ -499,9 +509,9 @@
 
         total = heads_total[...]
         for upper, start in enumerate((lower_start(t), upper_start(t))):
-            total = total + lax.dot_general(
+            total = total + jnp.dot(
                 tokens[t, upper], weight_buf[:, pl.ds(start, UNIT_WIDE)],
-                (((1,), (1,)), ((), ())), preferred_element_type=jnp.float32,
+                preferred_element_type=jnp.float32,
             )
         heads_total[...] = total
         for upper, target in enumerate((t // 2, GROUPS - 1 - t // 2)):

time: 129 us -> 129 us (level)
  no operation moved by 1% of the time
where the time goes in v2:
time: 129 us
  Pallas kernels  128 us (99%)
    pallas_call x1, Pallas kernels, fused(): pl.pallas_call(boundary_kernel, out_shape=(jax.ShapeDtypeStruct(heads.sha...  125 us
    pallas_call x1, Pallas kernels, delivered(): pl.pallas_call(deliver_kernel, out_shape=tuple((jax.ShapeDtypeStruct(resu...  3.24 us

profile of v2, /device:TPU:2, one launch (start us, length us, event | category | flops | bytes accessed | tf_op | source)
XLA Modules:
  0.0 129.1 jit_solution(6892148420628012972)
XLA Ops:
  0.6 125.2 %boundary.1 = (bf16[384,512]{1,0:T(8,128)(2,1)}, f32[1024,512]{1,0:T(8,128)}, bf16[24,8192]{1,0:T(8,128)(2,1)}, f32[1,8192]{1,0:T(1,128)}) custom-call(bf16[384,512]{1,0:T(8,128)(2,1)} %bitcast.7, bf16[512,8192]{1,0:T(8,128)(2,1)} %bitcast.6, bf16[24,8192]{1,0:T(8,128)(2,1)} %residual_in.1, f32[1,8192]{1,0:T(1,128)} %bitcast.8), custom_call_target="tpu_custom_call" | custom-call | tf_op jit(solution)/shard_map/boundary/pallas_call | solution.py:714
  125.8 3.2 %deliver.1 = (bf16[384,512]{1,0:T(8,128)(2,1)}, f32[1024,512]{1,0:T(8,128)}, bf16[24,8192]{1,0:T(8,128)(2,1)}, f32[1,8192]{1,0:T(1,128)}) custom-call(bf16[384,512]{1,0:T(8,128)(2,1)} %get-tuple-element.12.refs_0_, f32[1024,512]{1,0:T(8,128)} %get-tuple-element.13.refs_1_, bf16[24,8192]{1,0:T(8,128)(2,1)} %get-tuple-element.14.refs_2_, ...), custom_call_target="tpu_custom_call" | custom-call | tf_op jit(solution)/shard_map/deliver/pallas_call | solution.py:697

commit v3 on v0

--- a/solution.py
+++ b/solution.py
@@ -186,14 +186,19 @@
         held = heads_all.at[slot]
         return remote(held, held, heads_send.at[slot], heads_recv.at[slot], sibling)
 
-    def pass_heads():
-        @pl.when(jnp.logical_or(z == 0, z == SIDE - 1))
-        def _():
-            for j in range(SIDE - 1):
-                heads_arrived(2 * j + core)
-
+    def pass_heads(late):
         for j in range(SIDE - 1):
-            passed_heads(j).start()
+            far = jnp.logical_or(
+                jnp.logical_and(z == 0, j == SIDE - 2), jnp.logical_and(z == SIDE - 1, j == 0)
+            )
+
+            @pl.when(far if late else jnp.logical_not(far))
+            def _():
+                @pl.when(jnp.logical_or(z == 0, z == SIDE - 1))
+                def _():
+                    heads_arrived(2 * j + core)
+
+                passed_heads(j).start()
 
     def send_heads():
         heads_t[...] = heads[...].T
@@ -314,19 +319,19 @@
             def _():
                 stage(n - late)
 
-        @pl.when(n == 1)
-        def _():
-            send_heads()
-
-        @pl.when(n == UNITS - 1)
-        def _():
-            each_relay((1,), pass_relay)
+        for away, at in ((1, 4), (2, 9)):
+
+            @pl.when(n == at)
+            def _():
+                each_relay((away,), pass_relay)
 
         return carry
 
+    send_heads()
     residual_load.wait()
     gain_load.wait()
     lax.fori_loop(0, UNITS + len(stages) - 1, reduce_turn, 0)
+    pass_heads(False)
     heads_total[...] = jnp.zeros_like(heads_total)
     grads_t[...] = jnp.zeros_like(grads_t)
 
@@ -581,9 +586,9 @@
             pass_on(gather_columns, column_recv, q - UNITS)
 
     def gather_turn(n, carry):
-        @pl.when(n == 5)
-        def _():
-            pass_heads()
+        @pl.when(n == 4)
+        def _():
+            pass_heads(True)
 
         for step in range(GAIN_STEPS + 1):
 
@@ -641,7 +646,6 @@
         return carry
 
     own_grad_store.start()
-    each_relay((2,), pass_relay)
     lax.fori_loop(0, UNITS + FAR_UNITS + 5, gather_turn, 0)
     finish_grads((2, 3))
 

time: 129 us -> 134 us (1.039)
  Pallas kernels: 128 us -> 133 us
    pallas_call x1, Pallas kernels: 125 us -> 130 us  [fused(): pl.pallas_call(boundary_kernel, out_shape=(jax.ShapeDtypeStruct(heads.sha...]
where the time goes in v3:
time: 134 us
  Pallas kernels  133 us (99%)
    pallas_call x1, Pallas kernels, fused(): pl.pallas_call(boundary_kernel, out_shape=(jax.ShapeDtypeStruct(heads.sha...  130 us
    pallas_call x1, Pallas kernels, delivered(): pl.pallas_call(deliver_kernel, out_shape=tuple((jax.ShapeDtypeStruct(resu...  3.24 us

profile of v3, /device:TPU:2, one launch (start us, length us, event | category | flops | bytes accessed | tf_op | source)
XLA Modules:
  0.0 133.6 jit_solution(3755235174078985398)
XLA Ops:
  0.6 129.8 %boundary.1 = (bf16[384,512]{1,0:T(8,128)(2,1)}, f32[1024,512]{1,0:T(8,128)}, bf16[24,8192]{1,0:T(8,128)(2,1)}, f32[1,8192]{1,0:T(1,128)}) custom-call(bf16[384,512]{1,0:T(8,128)(2,1)} %bitcast.7, bf16[512,8192]{1,0:T(8,128)(2,1)} %bitcast.6, bf16[24,8192]{1,0:T(8,128)(2,1)} %residual_in.1, f32[1,8192]{1,0:T(1,128)} %bitcast.8), custom_call_target="tpu_custom_call" | custom-call | tf_op jit(solution)/shard_map/boundary/pallas_call | solution.py:708
  130.4 3.2 %deliver.1 = (bf16[384,512]{1,0:T(8,128)(2,1)}, f32[1024,512]{1,0:T(8,128)}, bf16[24,8192]{1,0:T(8,128)(2,1)}, f32[1,8192]{1,0:T(1,128)}) custom-call(bf16[384,512]{1,0:T(8,128)(2,1)} %get-tuple-element.12.refs_0_, f32[1024,512]{1,0:T(8,128)} %get-tuple-element.13.refs_1_, bf16[24,8192]{1,0:T(8,128)(2,1)} %get-tuple-element.14.refs_2_, ...), custom_call_target="tpu_custom_call" | custom-call | tf_op jit(solution)/shard_map/deliver/pallas_call | solution.py:691

commit v4 on v0

--- a/solution.py
+++ b/solution.py
@@ -186,14 +186,18 @@
         held = heads_all.at[slot]
         return remote(held, held, heads_send.at[slot], heads_recv.at[slot], sibling)
 
-    def pass_heads():
-        @pl.when(jnp.logical_or(z == 0, z == SIDE - 1))
-        def _():
-            for j in range(SIDE - 1):
-                heads_arrived(2 * j + core)
-
+    def pass_heads(neighbours):
         for j in range(SIDE - 1):
-            passed_heads(j).start()
+            origin = (z + 1 + j) % SIDE
+            near = jnp.logical_or(origin == z + 1, origin == z - 1)
+
+            @pl.when(near if neighbours else jnp.logical_not(near))
+            def _():
+                @pl.when(jnp.logical_or(z == 0, z == SIDE - 1))
+                def _():
+                    heads_arrived(2 * j + core)
+
+                passed_heads(j).start()
 
     def send_heads():
         heads_t[...] = heads[...].T
@@ -327,6 +331,7 @@
     residual_load.wait()
     gain_load.wait()
     lax.fori_loop(0, UNITS + len(stages) - 1, reduce_turn, 0)
+    pass_heads(True)
     heads_total[...] = jnp.zeros_like(heads_total)
     grads_t[...] = jnp.zeros_like(grads_t)
 
@@ -583,7 +588,7 @@
     def gather_turn(n, carry):
         @pl.when(n == 5)
         def _():
-            pass_heads()
+            pass_heads(False)
 
         for step in range(GAIN_STEPS + 1):
 
@@ -671,8 +676,16 @@
 def deliver_kernel(*refs):
     results, outputs, held = refs[:4], refs[4:8], refs[8:12]
     load_sem, store_sem = refs[12:]
-    loads = [pltpu.make_async_copy(results[at], held[at], load_sem.at[at]) for at in range(4)]
-    stores = [pltpu.make_async_copy(held[at], outputs[at], store_sem.at[at]) for at in range(4)]
+    pieces = [(1, pl.ds(block * WIDE, WIDE)) for block in range(SIDE)]
+    pieces += [(at, pl.ds(0, results[at].shape[0])) for at in (0, 2, 3)]
+
+    def copies(sources, targets, sems):
+        return [
+            pltpu.make_async_copy(sources[at].at[rows], targets[at].at[rows], sems.at[i])
+            for i, (at, rows) in enumerate(pieces)
+        ]
+
+    loads, stores = copies(results, held, load_sem), copies(held, outputs, store_sem)
     for load in loads:
         load.start()
     for load, store in zip(loads, stores):
@@ -690,7 +703,7 @@
         in_specs=[hbm] * 4,
         out_specs=(hbm,) * 4,
         scratch_shapes=[pltpu.VMEM(result.shape, result.dtype) for result in results]
-        + [pltpu.SemaphoreType.DMA((4,))] * 2,
+        + [pltpu.SemaphoreType.DMA((SIDE + 3,))] * 2,
         name="deliver",
     )(*results)
 

time: 129 us -> 129 us (level)
  no operation moved by 1% of the time
where the time goes in v4:
time: 129 us
  Pallas kernels  128 us (99%)
    pallas_call x1, Pallas kernels, fused(): pl.pallas_call(boundary_kernel, out_shape=(jax.ShapeDtypeStruct(heads.sha...  125 us
    pallas_call x1, Pallas kernels, delivered(): pl.pallas_call(deliver_kernel, out_shape=tuple((jax.ShapeDtypeStruct(resu...  2.73 us

profile of v4, /device:TPU:2, one launch (start us, length us, event | category | flops | bytes accessed | tf_op | source)
XLA Modules:
  0.0 128.6 jit_solution(8180540333841232579)
XLA Ops:
  0.6 125.2 %boundary.1 = (bf16[384,512]{1,0:T(8,128)(2,1)}, f32[1024,512]{1,0:T(8,128)}, bf16[24,8192]{1,0:T(8,128)(2,1)}, f32[1,8192]{1,0:T(1,128)}) custom-call(bf16[384,512]{1,0:T(8,128)(2,1)} %bitcast.7, bf16[512,8192]{1,0:T(8,128)(2,1)} %bitcast.6, bf16[24,8192]{1,0:T(8,128)(2,1)} %residual_in.1, f32[1,8192]{1,0:T(1,128)} %bitcast.8), custom_call_target="tpu_custom_call" | custom-call | tf_op jit(solution)/shard_map/boundary/pallas_call | solution.py:717
  125.8 2.7 %deliver.1 = (bf16[384,512]{1,0:T(8,128)(2,1)}, f32[1024,512]{1,0:T(8,128)}, bf16[24,8192]{1,0:T(8,128)(2,1)}, f32[1,8192]{1,0:T(1,128)}) custom-call(bf16[384,512]{1,0:T(8,128)(2,1)} %get-tuple-element.12.refs_0_, f32[1024,512]{1,0:T(8,128)} %get-tuple-element.13.refs_1_, bf16[24,8192]{1,0:T(8,128)(2,1)} %get-tuple-element.14.refs_2_, ...), custom_call_target="tpu_custom_call" | custom-call | tf_op jit(solution)/shard_map/deliver/pallas_call | solution.py:700

commit v5 on v4

--- a/solution.py
+++ b/solution.py
@@ -310,19 +310,20 @@
         return jnp.logical_and(value >= 0, value < count)
 
     stages = (multiply, near_first, far_second, near_second, finish)
+    APART = 2
 
     def reduce_turn(n, carry):
-        for late, stage in enumerate(stages):
-
-            @pl.when(within(n - late, UNITS))
+        for at, stage in enumerate(stages):
+
+            @pl.when(within(n - APART * at, UNITS))
             def _():
-                stage(n - late)
+                stage(n - APART * at)
 
         @pl.when(n == 1)
         def _():
             send_heads()
 
-        @pl.when(n == UNITS - 1)
+        @pl.when(n == UNITS + 2)
         def _():
             each_relay((1,), pass_relay)
 
@@ -330,7 +331,7 @@
 
     residual_load.wait()
     gain_load.wait()
-    lax.fori_loop(0, UNITS + len(stages) - 1, reduce_turn, 0)
+    lax.fori_loop(0, UNITS + APART * (len(stages) - 1), reduce_turn, 0)
     pass_heads(True)
     heads_total[...] = jnp.zeros_like(heads_total)
     grads_t[...] = jnp.zeros_like(grads_t)
@@ -586,13 +587,13 @@
             pass_on(gather_columns, column_recv, q - UNITS)
 
     def gather_turn(n, carry):
-        @pl.when(n == 5)
+        @pl.when(n == 8)
         def _():
             pass_heads(False)
 
         for step in range(GAIN_STEPS + 1):
 
-            @pl.when(n == step + 1)
+            @pl.when(n == step + 6)
             def _():
                 if step > 0:
                     gain_copy(step - 1).wait_recv()
@@ -603,23 +604,23 @@
                     gain_done[...] = gain_own[GAIN_STEPS] * grad_scale
                     gain_store.start()
 
-        @pl.when(within(n + 1 - UNITS, FAR_UNITS))
-        def _():
-            p = n + 1 - UNITS
+        @pl.when(within(n + 2 - UNITS, FAR_UNITS))
+        def _():
+            p = n + 2 - UNITS
             wait_arrived(gather_sizes[1], exchange_recv.at[p])
             for h in range(2):
                 gather_columns(p, h, 0).start()
                 gather_columns(p, h, 1).start()
 
-        @pl.when(n == UNITS + FAR_UNITS + 4)
+        @pl.when(n == UNITS + FAR_UNITS + 7)
         def _():
             finish_grads((0, 1))
 
         gather_stage(n, 0)
-        gather_stage(n - 4, 2)
-        gather_stage(n - 2, 1)
-        gather_stage(n - 5, 3)
-        done = n - 5
+        gather_stage(n - 6, 2)
+        gather_stage(n - 3, 1)
+        gather_stage(n - 8, 3)
+        done = n - 8
 
         @pl.when(within(done, UNITS))
         def _():
@@ -647,7 +648,7 @@
 
     own_grad_store.start()
     each_relay((2,), pass_relay)
-    lax.fori_loop(0, UNITS + FAR_UNITS + 5, gather_turn, 0)
+    lax.fori_loop(0, UNITS + FAR_UNITS + 8, gather_turn, 0)
     finish_grads((2, 3))
 
     def reduce_sent(u, carry):

time: 129 us -> 130 us (level)
  no operation moved by 1% of the time
where the time goes in v5:
time: 130 us; the launch traced here: 129 us
  Pallas kernels  129 us (99%)
    pallas_call x1, Pallas kernels, fused(): pl.pallas_call(boundary_kernel, out_shape=(jax.ShapeDtypeStruct(heads.sha...  126 us
    pallas_call x1, Pallas kernels, delivered(): pl.pallas_call(deliver_kernel, out_shape=tuple((jax.ShapeDtypeStruct(resu...  2.73 us

profile of v5, /device:TPU:2, one launch (start us, length us, event | category | flops | bytes accessed | tf_op | source)
XLA Modules:
  0.0 129.3 jit_solution(16973046065952300902)
XLA Ops:
  0.6 125.9 %boundary.1 = (bf16[384,512]{1,0:T(8,128)(2,1)}, f32[1024,512]{1,0:T(8,128)}, bf16[24,8192]{1,0:T(8,128)(2,1)}, f32[1,8192]{1,0:T(1,128)}) custom-call(bf16[384,512]{1,0:T(8,128)(2,1)} %bitcast.7, bf16[512,8192]{1,0:T(8,128)(2,1)} %bitcast.6, bf16[24,8192]{1,0:T(8,128)(2,1)} %residual_in.1, f32[1,8192]{1,0:T(1,128)} %bitcast.8), custom_call_target="tpu_custom_call" | custom-call | tf_op jit(solution)/shard_map/boundary/pallas_call | solution.py:718
  126.5 2.7 %deliver.1 = (bf16[384,512]{1,0:T(8,128)(2,1)}, f32[1024,512]{1,0:T(8,128)}, bf16[24,8192]{1,0:T(8,128)(2,1)}, f32[1,8192]{1,0:T(1,128)}) custom-call(bf16[384,512]{1,0:T(8,128)(2,1)} %get-tuple-element.12.refs_0_, f32[1024,512]{1,0:T(8,128)} %get-tuple-element.13.refs_1_, bf16[24,8192]{1,0:T(8,128)(2,1)} %get-tuple-element.14.refs_2_, ...), custom_call_target="tpu_custom_call" | custom-call | tf_op jit(solution)/shard_map/deliver/pallas_call | solution.py:701

commit v6 on v5

--- a/solution.py
+++ b/solution.py
@@ -310,20 +310,19 @@
         return jnp.logical_and(value >= 0, value < count)
 
     stages = (multiply, near_first, far_second, near_second, finish)
-    APART = 2
 
     def reduce_turn(n, carry):
-        for at, stage in enumerate(stages):
-
-            @pl.when(within(n - APART * at, UNITS))
+        for late, stage in enumerate(stages):
+
+            @pl.when(within(n - late, UNITS))
             def _():
-                stage(n - APART * at)
+                stage(n - late)
 
         @pl.when(n == 1)
         def _():
             send_heads()
 
-        @pl.when(n == UNITS + 2)
+        @pl.when(n == UNITS - 1)
         def _():
             each_relay((1,), pass_relay)
 
@@ -331,7 +330,7 @@
 
     residual_load.wait()
     gain_load.wait()
-    lax.fori_loop(0, UNITS + APART * (len(stages) - 1), reduce_turn, 0)
+    lax.fori_loop(0, UNITS + len(stages) - 1, reduce_turn, 0)
     pass_heads(True)
     heads_total[...] = jnp.zeros_like(heads_total)
     grads_t[...] = jnp.zeros_like(grads_t)

time: 130 us -> 124 us (0.954)
  Pallas kernels: 129 us -> 122 us
    pallas_call x1, Pallas kernels: 126 us -> 119 us  [fused(): pl.pallas_call(boundary_kernel, out_shape=(jax.ShapeDtypeStruct(heads.sha...]
where the time goes in v6:
time: 124 us; the launch traced here: 123 us
  Pallas kernels  122 us (98%)
    pallas_call x1, Pallas kernels, fused(): pl.pallas_call(boundary_kernel, out_shape=(jax.ShapeDtypeStruct(heads.sha...  119 us
    pallas_call x1, Pallas kernels, delivered(): pl.pallas_call(deliver_kernel, out_shape=tuple((jax.ShapeDtypeStruct(resu...  2.73 us

profile of v6, /device:TPU:2, one launch (start us, length us, event | category | flops | bytes accessed | tf_op | source)
XLA Modules:
  0.0 122.5 jit_solution(16267299956753422694)
XLA Ops:
  0.6 119.2 %boundary.1 = (bf16[384,512]{1,0:T(8,128)(2,1)}, f32[1024,512]{1,0:T(8,128)}, bf16[24,8192]{1,0:T(8,128)(2,1)}, f32[1,8192]{1,0:T(1,128)}) custom-call(bf16[384,512]{1,0:T(8,128)(2,1)} %bitcast.7, bf16[512,8192]{1,0:T(8,128)(2,1)} %bitcast.6, bf16[24,8192]{1,0:T(8,128)(2,1)} %residual_in.1, f32[1,8192]{1,0:T(1,128)} %bitcast.8), custom_call_target="tpu_custom_call" | custom-call | tf_op jit(solution)/shard_map/boundary/pallas_call | solution.py:717
  119.8 2.7 %deliver.1 = (bf16[384,512]{1,0:T(8,128)(2,1)}, f32[1024,512]{1,0:T(8,128)}, bf16[24,8192]{1,0:T(8,128)(2,1)}, f32[1,8192]{1,0:T(1,128)}) custom-call(bf16[384,512]{1,0:T(8,128)(2,1)} %get-tuple-element.12.refs_0_, f32[1024,512]{1,0:T(8,128)} %get-tuple-element.13.refs_1_, bf16[24,8192]{1,0:T(8,128)(2,1)} %get-tuple-element.14.refs_2_, ...), custom_call_target="tpu_custom_call" | custom-call | tf_op jit(solution)/shard_map/deliver/pallas_call | solution.py:700
